TPU v7x, 256 devices: a whole 4x4x8 slice. The times are simulated.
256 devices in a mesh: wide: 32 (over x, y, core), narrow: 8 (over z).
Axes of the slice: x: 4, y: 4, z: 8, core: 2. Of those that a mesh axis runs over, the one named last changes fastest.
Arguments:
- tokens: bfloat16 [2048, 7168], P(('wide', 'narrow')), may hold values from -6 to 6
- routes: int32 [2048, 8], P(('wide', 'narrow')), may hold values from 0 to 31, all different within a row; in each aligned block of 8 rows (0 to 7, 8 to 15, ...) at most 4 rows name the same one
- gates: float32 [2048, 8], P(('wide', 'narrow')), may hold values from 0.05 to 0.5
- fallback: int32 [32], replicated, may hold values from 0 to 31, each once
- w_gate: bfloat16 [32, 7168, 2048], P('wide', 'narrow'), may hold values from -0.0625 to 0.0625
- w_up: bfloat16 [32, 7168, 2048], P('wide', 'narrow'), may hold values from -0.0625 to 0.0625
- w_down: bfloat16 [32, 2048, 7168], P('wide', None, 'narrow'), may hold values from -0.125 to 0.125
Outputs:
- mixed: bfloat16 [2048, 7168], P(('wide', 'narrow'))
Inputs may be any that keep to these rules, and one draw needn't show every extreme that they name: `routes`: each row names 8 different experts. Among the 8 rows of one device no expert is named more than 2 * 2 times, and in every draw some expert is named exactly 2 * 2 times by some device's rows. `fallback`: each expert appears once.
All inputs are finite; a program needn't handle non-finite values.
Results may differ from a plain program's by a relative error of at most 0.029.
Values may be sent and summed in bfloat16 or wider, within the bound.
A program may use at most 128 MiB of HBM per device.

v0:
```python
import jax
import jax.numpy as jnp
from jax import lax
from jax.sharding import PartitionSpec as P


def on_device(tokens, routes, gates, fallback, w_gate, w_up, w_down):
    experts = lax.axis_size("wide")
    narrow = lax.axis_size("narrow")
    tok_rows, width = tokens.shape
    chosen_count = routes.shape[1]
    capacity = min(tok_rows // 2, tok_rows * chosen_count // experts)
    slots = 2 * capacity
    block = width // narrow
    expert_ids = jnp.arange(experts, dtype=jnp.int32)
    matched = routes[:, :, None] == expert_ids[None, None, :]
    hits = jnp.sum(matched.astype(jnp.int32), axis=1)
    weight_of = jnp.sum(jnp.where(matched, gates[:, :, None], 0.0), axis=1)
    ranks = jnp.cumsum(hits, axis=0) - hits
    slot_ids = jnp.arange(slots, dtype=jnp.int32)
    placed = ((hits[:, :, None] == 1) & (ranks[:, :, None] == slot_ids[None, None, :])).astype(
        jnp.float32
    )
    redirect = (fallback[:, None] == expert_ids[None, :]).astype(jnp.float32)

    def arrange(table):
        moved = jnp.einsum(
            "tes,ed->tds", table[:, :, capacity:], redirect, precision=lax.Precision.HIGHEST
        )
        return jnp.concatenate([table[:, :, :capacity], moved], axis=2)

    layout = arrange(placed)
    selector = layout.astype(jnp.bfloat16).reshape(tok_rows, experts * slots)
    pieces = tokens.reshape(tok_rows, narrow, block)
    outgoing = jnp.einsum(
        "ts,tnd->nsd", selector, pieces, preferred_element_type=jnp.float32
    ).astype(jnp.bfloat16)
    outgoing = outgoing.reshape(narrow, experts, slots, block)
    arrived = lax.all_to_all(
        lax.all_to_all(outgoing, "wide", split_axis=1, concat_axis=2, tiled=True),
        "narrow",
        split_axis=0,
        concat_axis=2,
        tiled=True,
    )
    inputs = arrived.reshape(-1, block)
    gate_w = w_gate[0]
    up_w = w_up[0]
    down_w = w_down[0]
    gate_part = jnp.dot(inputs, gate_w, preferred_element_type=jnp.float32)
    up_part = jnp.dot(inputs, up_w, preferred_element_type=jnp.float32)
    gate_share, up_share = (
        lax.psum_scatter(
            gate_part.astype(jnp.bfloat16), "narrow", scatter_dimension=1, tiled=True
        ).astype(jnp.float32),
        lax.psum_scatter(
            up_part.astype(jnp.bfloat16), "narrow", scatter_dimension=1, tiled=True
        ).astype(jnp.float32),
    )
    hidden = (jax.nn.silu(gate_share) * up_share).astype(jnp.bfloat16)
    output = jnp.dot(
        lax.all_gather(hidden, "narrow", axis=1, tiled=True),
        down_w,
        preferred_element_type=jnp.float32,
    ).astype(jnp.bfloat16)
    going_back = output.reshape(narrow, experts, slots, block)
    returned = lax.all_to_all(
        lax.all_to_all(going_back, "wide", split_axis=1, concat_axis=1, tiled=True),
        "narrow",
        split_axis=0,
        concat_axis=0,
        tiled=True,
    )
    combine = arrange(placed * weight_of[:, :, None]).reshape(tok_rows, experts * slots)
    values = returned.reshape(narrow, experts * slots, block).astype(jnp.float32)
    mixed = jnp.einsum("ts,nsd->tnd", combine, values, precision=lax.Precision.HIGHEST)
    return mixed.reshape(tok_rows, width).astype(jnp.bfloat16)


def solution(mesh):
    placed = (
        P(("wide", "narrow"), None),
        P(("wide", "narrow"), None),
        P(("wide", "narrow"), None),
        P(),
        P("wide", "narrow", None),
        P("wide", "narrow", None),
        P("wide", None, "narrow"),
    )
    return jax.shard_map(
        on_device,
        mesh=mesh,
        in_specs=placed,
        out_specs=P(("wide", "narrow"), None),
        check_vma=False,
    )
```

profile of v0, /device:TPU:1, one launch (start us, length us, event | category | flops | bytes accessed | tf_op | source)
XLA Modules:
  0.0 390.3 jit_solution(4963246133233776765)
XLA Ops:
  6.5 0.8 convert_reduce_fusion
  7.4 0.8 select_reduce_fusion
  8.2 0.8 fusion.7
  9.2 1.9 convert_bitcast_fusion
  11.1 3.1 reshape.55
  14.2 0.6 copy.44
  14.8 33.9 %all_to_all.31 = bf16[8,32,4,896]{3,2,0,1:T(4,128)(2,1)S(1)} all-to-all(bf16[8,32,4,896]{3,2,0,1:T(4,128)(2,1)S(1)} %copy.44), channel_id=1, replica_groups=mesh['wide'=32,'narrow'=8] {'wide'}, dimensions={1} | all-to-all | bytes 3670016 | tf_op jit(solution)/shard_map/all_to_all | solution.py:40
  49.3 54.3 %all_to_all.32 = bf16[8,1,128,896]{3,2,1,0:T(8,128)(2,1)S(1)} all-to-all(bf16[8,1,128,896]{3,2,1,0:T(8,128)(2,1)S(1)} %copy.46), channel_id=1, replica_groups=mesh['wide'=32,'narrow'=8] {'narrow'}, dimensions={0} | all-to-all | bytes 3670016 | tf_op jit(solution)/shard_map/all_to_all | solution.py:39
  103.6 6.0 %convolution_convert_fusion.2 = bf16[1024,2048]{1,0:T(8,128)(2,1)} fusion(bf16[1024,896]{1,0:T(8,128)(2,1)S(1)} %bitcast.43, bf16[1,896,2048]{2,1,0:T(8,128)(2,1)S(1)} %copy-done.1), kind=kOutput, calls=%fused_computation.2 | convolution fusion | flops 3760193536 | bytes 9699328 | tf_op jit(solution)/shard_map/dot_general | solution.py:50
  109.7 8.1 %convolution_convert_fusion.1 = bf16[1024,2048]{1,0:T(8,128)(2,1)} fusion(bf16[1024,896]{1,0:T(8,128)(2,1)S(1)} %bitcast.44, bf16[1,896,2048]{2,1,0:T(8,128)(2,1)} %param.12), kind=kOutput, calls=%fused_computation.1 | convolution fusion | flops 3760193536 | bytes 9699328 | tf_op jit(solution)/shard_map/dot_general | solution.py:51
  117.9 39.8 %reduce-scatter.3.cloned.1.call-done = bf16[1024,256]{1,0:T(8,128)(2,1)} async-done(((bf16[1024,2048]{1,0:T(8,128)(2,1)}), bf16[1024,256]{1,0:T(8,128)(2,1)}) %reduce-scatter.3.cloned.1.call-update) | async-done | bytes 524304 | tf_op jit(solution)/shard_map/reduce_scatter | solution.py:53
  157.7 56.5 %reduce-scatter.5.cloned.1.call-done = bf16[1024,256]{1,0:T(8,128)(2,1)} async-done(((bf16[1024,2048]{1,0:T(8,128)(2,1)}), bf16[1024,256]{1,0:T(8,128)(2,1)}) %reduce-scatter.5.cloned.1.call-update) | async-done | bytes 524304 | tf_op jit(solution)/shard_map/reduce_scatter | solution.py:56
  214.2 2.3 fusion.12
  216.6 58.4 %all-gather.2.cloned.1.call-done = bf16[1024,2048]{1,0:T(8,128)(2,1)} async-done(((bf16[1024,256]{1,0:T(8,128)(2,1)}), bf16[1024,2048]{1,0:T(8,128)(2,1)}) %all-gather.2.cloned.1.call-update) | async-done | bytes 4194320 | tf_op jit(solution)/shard_map/all_gather | solution.py:62
  275.0 9.1 %fusion.4 = bf16[1024,896]{1,0:T(8,128)(2,1)} fusion(bf16[1024,2048]{1,0:T(8,128)(2,1)} %all-gather.2.cloned.1.call-done, bf16[1,2048,896]{2,1,0:T(8,128)(2,1)} %param.13), kind=kOutput, calls=%fused_computation.8 | convolution fusion | flops 3759013888 | bytes 9699328 | tf_op jit(solution)/shard_map/dot_general | solution.py:61
  284.1 3.1 reshape.57
  287.2 0.6 copy.47
  287.8 35.4 %all_to_all.33 = bf16[8,32,4,896]{3,2,0,1:T(4,128)(2,1)S(1)} all-to-all(bf16[8,32,4,896]{3,2,0,1:T(4,128)(2,1)S(1)} %copy.47), channel_id=1, replica_groups=mesh['wide'=32,'narrow'=8] {'wide'}, dimensions={1} | all-to-all | bytes 3670016 | tf_op jit(solution)/shard_map/all_to_all | solution.py:68
  323.2 2.0 copy.48
  325.2 4.3 %all-to-all-start.3 = ((bf16[8,32,4,896]{3,2,1,0:T(4,128)(2,1)}), bf16[8,32,4,896]{3,2,1,0:T(4,128)(2,1)S(1)}, u32[]{:S(2)}, u32[]{:S(2)}) async-start(bf16[8,32,4,896]{3,2,1,0:T(4,128)(2,1)} %copy.48), calls=%async_computation.5 | async-start | bytes 3670016 | tf_op jit(solution)/shard_map/all_to_all | solution.py:67
  329.8 45.8 %all-to-all-done.3 = bf16[8,32,4,896]{3,2,1,0:T(4,128)(2,1)S(1)} async-done(((bf16[8,32,4,896]{3,2,1,0:T(4,128)(2,1)}), bf16[8,32,4,896]{3,2,1,0:T(4,128)(2,1)S(1)}, u32[]{:S(2)}, u32[]{:S(2)}) %all-to-all-start.3) | async-done | bytes 1835040 | tf_op jit(solution)/shard_map/all_to_all | solution.py:67
  375.6 2.9 copy.49
  378.4 3.1 copy.50
  381.6 2.2 convolution_convert_fusion
  (25 shorter events, 1.1 us)
Async XLA Ops:
  6.5 2.7 copy-start
  6.5 151.2 %reduce-scatter.3.cloned.1.call-start = ((), (), s32[]{:S(2)}) async-start(), calls=%async_computation.6 | async-start | bytes 4718592 | tf_op jit(solution)/shard_map/reduce_scatter | solution.py:53
  49.3 54.3 %copy-start.1 = (bf16[1,896,2048]{2,1,0:T(8,128)(2,1)S(1)}, bf16[1,896,2048]{2,1,0:T(8,128)(2,1)}, u32[]{:S(2)}) copy-start(bf16[1,896,2048]{2,1,0:T(8,128)(2,1)} %param.11) | copy-start | bytes 11010052
  109.7 104.6 %reduce-scatter.5.cloned.1.call-start = ((), (), s32[]{:S(2)}) async-start(), calls=%async_computation.7 | async-start | bytes 4718592 | tf_op jit(solution)/shard_map/reduce_scatter | solution.py:56
  117.8 157.2 %all-gather.2.cloned.1.call-start = ((), (), s32[]{:S(2)}) async-start(), calls=%async_computation.8 | async-start | bytes 4718592 | tf_op jit(solution)/shard_map/all_gather | solution.py:62
  325.2 4.3 %copy-start.2 = (s32[32]{0:T(128)S(1)}, s32[32]{0:T(128)}, u32[]{:S(2)}) copy-start(s32[32]{0:T(128)} %param.10) | copy-start | bytes 388
  325.2 50.4 %all-to-all-start.3 = ((bf16[8,32,4,896]{3,2,1,0:T(4,128)(2,1)}), bf16[8,32,4,896]{3,2,1,0:T(4,128)(2,1)S(1)}, u32[]{:S(2)}, u32[]{:S(2)}) async-start(bf16[8,32,4,896]{3,2,1,0:T(4,128)(2,1)} %copy.48), calls=%async_computation.5 | async-start | bytes 3670016 | tf_op jit(solution)/shard_map/all_to_all | solution.py:67
Sparse Core Ops, SparseCore 0:
  109.8 47.8 reduce-scatter.2
  160.3 53.9 reduce-scatter.4
  216.7 58.2 all-gather.1
where the time goes:
time: 391 us; the launch traced here: 390 us
  waiting for transfers between devices  201 us (51%)
  blocking collectives  124 us (32%)
  matrix products  28.3 us (7%)
  local copies, waits for them, and re-layouts  16.2 us (4%)
  between operations  13.2 us (3%)
  starting transfers between devices  4.39 us (1%)
  other arithmetic  3.97 us (1%)
    all_gather x1, waiting for transfers between devices, on_device(): lax.all_gather(hidden, 'narrow', axis=1, tiled=True)  58.4 us
    reduce_scatter x1, waiting for transfers between devices, on_device(): lax.psum_scatter(up_part.astype(jnp.bfloat16), 'narrow', scatter_dimensio...  56.5 us
    all_to_all x1, blocking collectives, on_device(): lax.all_to_all(lax.all_to_all(outgoing, 'wide', split_axis=1, concat_axis...  54.3 us
    all_to_all x1, waiting for transfers between devices, on_device(): lax.all_to_all(lax.all_to_all(going_back, 'wide', split_axis=1, concat_ax...  45.8 us
    reduce_scatter x1, waiting for transfers between devices, on_device(): lax.psum_scatter(gate_part.astype(jnp.bfloat16), 'narrow', scatter_dimens...  39.8 us
    all_to_all x1, blocking collectives, on_device(): lax.all_to_all(going_back, 'wide', split_axis=1, concat_axis=1, tiled=True)  35.4 us
    all_to_all x1, blocking collectives, on_device(): lax.all_to_all(outgoing, 'wide', split_axis=1, concat_axis=2, tiled=True)  33.9 us
    dot_general x1, matrix products, on_device(): jnp.dot(lax.all_gather(hidden, 'narrow', axis=1, tiled=True), down_w, pre...  9.06 us
  transfers between devices with their start and end apart: 4, of which 4 were waited for; matrix products, arithmetic and copies ran while one was open for 2% of the time, Pallas kernels for 0%

commit v1 on v0

v1 whole, which is shorter than its diff:
```python
import functools

import jax
import jax.numpy as jnp
from jax import lax
from jax.experimental import pallas as pl
from jax.experimental.pallas import tpu as pltpu
from jax.sharding import PartitionSpec as P

F32 = jnp.float32
BF16 = jnp.bfloat16
NX, NY, NC, NZ = 4, 4, 2, 8
SIDE = 128
WIDE_LO = 512
SUBS = 4


def dot(a, b):
    return jnp.dot(a, b, preferred_element_type=F32)


class Copies:
    def __init__(self, send, recv):
        self.send, self.recv = send, recv
        self.used = 0
        self.started = []

    def slot(self):
        self.used += 1
        return self.used - 1

    def make(self, slot, src, dst, device):
        return pltpu.make_async_remote_copy(
            src_ref=src,
            dst_ref=dst,
            send_sem=self.send.at[slot],
            recv_sem=self.recv.at[slot],
            device_id=device,
            device_id_type=pl.DeviceIdType.MESH,
        )

    def go(self, slot, src, dst, device):
        copy = self.make(slot, src, dst, device)
        copy.start()
        self.started.append(copy)


def kernel(
    tok,
    wg_hbm,
    wu_hbm,
    wd_hbm,
    out,
    zin,
    g,
    x,
    sel,
    wcol,
    wg,
    wu,
    wd,
    first,
    part,
    hid,
    acc,
    c,
    core_in,
    ra1,
    ra2,
    rb1,
    rb2,
    zout,
    zback,
    load_sem,
    send,
    recv,
    rs_send,
    rs_recv,
    ag_send,
    ag_recv,
):
    wide, z = lax.axis_index("wide"), lax.axis_index("narrow")
    cc = lax.rem(wide, NC)
    yy = lax.rem(wide // NC, NY)
    xx = wide // (NC * NY)
    block = x.shape[1]
    rows = x.shape[0]
    half = rows // 2
    sub = half // SUBS
    cols = wg.shape[1] // NZ

    def at(px, py, pc):
        return (px * NY + py) * NC + pc

    def xs(k):
        return lax.rem(xx + k, NX)

    def ys(k):
        return lax.rem(yy + k, NY)

    def zs(k):
        return lax.rem(z + k, NZ)

    xdev = {1: (at(xs(1), yy, cc), z), -1: (at(xs(3), yy, cc), z)}
    ydev = {1: (at(xx, ys(1), cc), z), -1: (at(xx, ys(3), cc), z)}
    mate = (at(xx, yy, 1 - cc), z)

    loads = [
        pltpu.make_async_copy(a, b, load_sem.at[i])
        for i, (a, b) in enumerate(((wg_hbm, wg), (wu_hbm, wu), (wd_hbm, wd)))
    ]
    for load in loads:
        load.start()

    barrier = pltpu.get_barrier_semaphore()
    peers = [xdev[1], xdev[-1], ydev[1], ydev[-1], mate] + [(wide, zs(k)) for k in range(1, NZ)]
    for peer in peers:
        pl.semaphore_signal(barrier, inc=1, device_id=peer, device_id_type=pl.DeviceIdType.MESH)
    pl.semaphore_wait(barrier, len(peers))

    copies = Copies(send, recv)

    zslots = {}
    for k in range(1, NZ):
        zslots[k] = copies.slot()
        copies.go(zslots[k], tok.at[zs(k)], zin.at[z], (wide, zs(k)))
    zin[z] = tok[z]
    for k in range(1, NZ):
        src = zs(NZ - k)
        copies.make(zslots[k], tok.at[src], zin.at[src], (wide, src)).wait_recv()
    arrived = zin[...].astype(F32)
    tokens_z = arrived.shape[0] * arrived.shape[1] // 2
    g[xx, yy, cc, :, :WIDE_LO] = arrived[:, :8, :].reshape(tokens_z, WIDE_LO).astype(BF16)
    g[xx, yy, cc, :, WIDE_LO:] = arrived[:, 8:, :].reshape(tokens_z, WIDE_LO).astype(BF16)

    def lane_a(pos):
        return lambda lo, n: g.at[pos, yy, cc, pl.ds(lo, n)]

    def lane_b(pos):
        return lambda lo, n: g.at[xx, pos, cc, pl.ds(32 + lo, n)]

    def plane_a(pos):
        return lambda lo, n: g.at[:, pos, cc, pl.ds(lo, n)]

    def plane_b(pos):
        return lambda lo, n: g.at[pos, :, cc, pl.ds(32 + lo, n)]

    def gather_start(region, step, dev):
        right, left = copies.slot(), copies.slot()
        own = region(step(0))(0, 32)
        copies.go(right, own, own, dev[1])
        copies.go(left, own, own, dev[-1])
        return right, left

    def gather_forward(region, step, dev, slots):
        right, left = copies.slot(), copies.slot()
        before, after = region(step(3)), region(step(1))
        copies.make(slots[0], before(0, 32), before(0, 32), dev[-1]).wait_recv()
        copies.go(right, before(0, 16), before(0, 16), dev[1])
        copies.make(slots[1], after(0, 32), after(0, 32), dev[1]).wait_recv()
        copies.go(left, after(16, 16), after(16, 16), dev[-1])
        return right, left

    def gather_end(region, step, dev, slots):
        far = region(step(2))
        copies.make(slots[0], far(0, 16), far(0, 16), dev[-1]).wait_recv()
        copies.make(slots[1], far(16, 16), far(16, 16), dev[1]).wait_recv()

    core_waits = []

    def to_mate(region, step, k):
        slot = copies.slot()
        copies.go(slot, region(step(k))(0, 32), region(step(k))(0, 32), mate)
        core_waits.append((slot, region, step, k))

    a1 = gather_start(lane_a, xs, xdev)
    b1 = gather_start(lane_b, ys, ydev)
    a2 = gather_forward(lane_a, xs, xdev, a1)
    b2 = gather_forward(lane_b, ys, ydev, b1)
    gather_end(lane_a, xs, xdev, a2)
    a3 = gather_start(plane_a, ys, ydev)
    gather_end(lane_b, ys, ydev, b2)
    b3 = gather_start(plane_b, xs, xdev)
    to_mate(plane_a, ys, 0)
    to_mate(plane_b, xs, 0)
    a4 = gather_forward(plane_a, ys, ydev, a3)
    b4 = gather_forward(plane_b, xs, xdev, b3)
    for k in (1, 3):
        to_mate(plane_a, ys, k)
        to_mate(plane_b, xs, k)
    gather_end(plane_a, ys, ydev, a4)
    to_mate(plane_a, ys, 2)
    gather_end(plane_b, xs, xdev, b4)
    to_mate(plane_b, xs, 2)
    other = {
        plane_a: lambda pos: g.at[:, pos, 1 - cc, pl.ds(0, 32)],
        plane_b: lambda pos: g.at[pos, :, 1 - cc, pl.ds(32, 32)],
    }
    for slot, region, step, k in core_waits:
        there = other[region](step(k))
        copies.make(slot, there, there, mate).wait_recv()

    batches = 8
    toks = NX * NY * NC * 64 // batches
    slots = rows // batches
    devs = slots // 4
    lane = lax.broadcasted_iota(jnp.int32, (toks, SIDE), 1)
    row = lax.broadcasted_iota(jnp.int32, (toks, SIDE), 0)
    mine = (lax.rem(lane, 32) == wide) & (lane < 96)
    square_r = lax.broadcasted_iota(jnp.int32, (toks, toks), 0)
    square_c = lax.broadcasted_iota(jnp.int32, (toks, toks), 1)
    lower = ((square_r // 8 == square_c // 8) & (square_c < square_r)).astype(F32).astype(BF16)
    for b in range(batches):
        here = g[b // 2, 2 * (b % 2) : 2 * (b % 2) + 2].reshape(toks, block + SIDE)
        weight = jnp.sum(
            jnp.where(mine, here[:, block:].astype(F32), 0.0), axis=1, keepdims=True
        )
        weight = jnp.broadcast_to(weight, (toks, SIDE))
        chosen = jnp.where(weight > 0.0, 1.0, 0.0)
        rank = dot(lower, chosen.astype(BF16)).astype(jnp.int32)
        place = rank * devs + row // 8
        pick = jnp.where((lane == place) & (weight > 0.0), 1.0, 0.0).astype(BF16)
        sel[b] = pick
        wcol[b] = weight
        taken = lax.dot_general(
            pick, here[:, :block], (((0,), (0,)), ((), ())), preferred_element_type=F32
        )
        x[b * slots : (b + 1) * slots, :] = taken.astype(BF16)

    loads[0].wait()
    loads[1].wait()
    zdev = ((wide, zs(1)), (wide, zs(NZ - 1)))

    def ring(s, d):
        return lax.rem(z + NZ - s, NZ) if d == 0 else lax.rem(z + s, NZ)

    def product(d, q, chunk):
        rows_here = x[pl.ds(pl.multiple_of(d * half + q * sub, sub), sub), :]
        at_cols = pl.ds(pl.multiple_of(chunk * cols, cols), cols)
        return dot(rows_here, wg[:, at_cols]), dot(rows_here, wu[:, at_cols])

    def rs_copy(d, s, q, src):
        return pltpu.make_async_remote_copy(
            src_ref=src,
            dst_ref=part.at[d, s, q],
            send_sem=rs_send.at[d, s, q],
            recv_sem=rs_recv.at[d, s, q],
            device_id=zdev[d],
            device_id_type=pl.DeviceIdType.MESH,
        )

    def ag_copy(d, s, q, chunk):
        here = hid.at[chunk, pl.ds(pl.multiple_of(d * half + q * sub, sub), sub)]
        return pltpu.make_async_remote_copy(
            src_ref=here,
            dst_ref=here,
            send_sem=ag_send.at[d, s, q],
            recv_sem=ag_recv.at[d, s, q],
            device_id=zdev[d],
            device_id_type=pl.DeviceIdType.MESH,
        )

    def each_sub(body):
        def step(q, carry):
            for d in range(2):
                body(d, q)
            return carry

        lax.fori_loop(0, SUBS, step, 0)

    def rs_first(d, q):
        gate, up = product(d, q, ring(1, d))
        first[d, q, :, :cols] = gate.astype(BF16)
        first[d, q, :, cols:] = up.astype(BF16)
        rs_copy(d, 0, q, first.at[d, q]).start()

    each_sub(rs_first)

    def rs_step(s, carry):
        def body(d, q):
            gate, up = product(d, q, ring(s + 1, d))
            rs_copy(d, s - 1, q, first.at[d, q]).wait_recv()
            here = part.at[d, s - 1, q]
            here[:, :cols] = (here[:, :cols].astype(F32) + gate).astype(BF16)
            here[:, cols:] = (here[:, cols:].astype(F32) + up).astype(BF16)
            rs_copy(d, s, q, here).start()

        each_sub(body)
        return carry

    lax.fori_loop(1, NZ - 1, rs_step, 0)
    loads[2].wait()

    def down(d, q, chunk):
        at_rows = pl.ds(pl.multiple_of(d * half + q * sub, sub), sub)
        at_cols = pl.ds(pl.multiple_of(chunk * cols, cols), cols)
        return at_rows, dot(hid[chunk, at_rows, :], wd[at_cols, :])

    def rs_last(d, q):
        gate, up = product(d, q, z)
        rs_copy(d, NZ - 2, q, first.at[d, q]).wait_recv()
        here = part.at[d, NZ - 2, q]
        gate = gate + here[:, :cols].astype(F32)
        up = up + here[:, cols:].astype(F32)
        hidden = gate / (1.0 + jnp.exp(-gate)) * up
        at_rows = pl.ds(pl.multiple_of(d * half + q * sub, sub), sub)
        hid[z, at_rows, :] = hidden.astype(BF16)
        ag_copy(d, 0, q, z).start()
        at_rows, value = down(d, q, z)
        acc[at_rows, :] = value

    each_sub(rs_last)

    def ag_step(s, carry):
        def body(d, q):
            chunk = ring(s, d)
            ag_copy(d, s - 1, q, chunk).wait_recv()
            ag_copy(d, s, q, chunk).start()
            at_rows, value = down(d, q, chunk)
            acc[at_rows, :] = acc[at_rows, :] + value

        each_sub(body)
        return carry

    lax.fori_loop(1, NZ - 1, ag_step, 0)

    core_slots = [copies.slot() for _ in range(NX)]
    for b in range(batches):
        d, q = b // SUBS, b % SUBS
        chunk = ring(NZ - 1, d)
        ag_copy(d, NZ - 2, q, chunk).wait_recv()
        at_rows, value = down(d, q, chunk)
        expert_out = (acc[at_rows, :] + value).astype(BF16)
        mixed = dot(sel[b], expert_out) * wcol[b][:, :1]
        c[b // 2, 2 * (b % 2) : 2 * (b % 2) + 2] = mixed.astype(BF16).reshape(2, NC, 64, block)
        if b % 2 == 1:
            copies.go(core_slots[b // 2], c.at[b // 2, :, 1 - cc], core_in.at[b // 2], mate)
    for px in range(NX):
        copies.make(core_slots[px], c.at[px, :, cc], core_in.at[px], mate).wait_recv()
        c[px, :, cc] = (c[px, :, cc].astype(F32) + core_in[px].astype(F32)).astype(BF16)

    def c_plane_a(pos, lo, n):
        return c.at[:, pos, cc, pl.ds(lo, n)]

    def c_plane_b(pos, lo, n):
        return c.at[pos, :, cc, pl.ds(32 + lo, n)]

    def c_lane_a(pos, lo, n):
        return c.at[pos, yy, cc, pl.ds(lo, n)]

    def c_lane_b(pos, lo, n):
        return c.at[xx, pos, cc, pl.ds(32 + lo, n)]

    def add_into(ref, other_ref):
        ref[...] = (ref[...].astype(F32) + other_ref[...].astype(F32)).astype(BF16)

    def scatter_start(region, step, dev, buf):
        right, left = copies.slot(), copies.slot()
        copies.go(right, region(step(2), 0, 16), buf.at[0], dev[1])
        copies.go(left, region(step(2), 16, 16), buf.at[1], dev[-1])
        return right, left

    def scatter_forward(region, step, dev, buf, buf2, slots):
        right, left = copies.slot(), copies.slot()
        copies.make(slots[0], region(step(2), 0, 16), buf.at[0], dev[-1]).wait_recv()
        add_into(region(step(1), 0, 16), buf.at[0])
        copies.go(right, region(step(1), 0, 32), buf2.at[0], dev[1])
        copies.make(slots[1], region(step(2), 16, 16), buf.at[1], dev[1]).wait_recv()
        add_into(region(step(3), 16, 16), buf.at[1])
        copies.go(left, region(step(3), 0, 32), buf2.at[1], dev[-1])
        return right, left

    def scatter_end(region, step, dev, buf2, slots):
        copies.make(slots[0], region(step(0), 0, 32), buf2.at[0], dev[-1]).wait_recv()
        copies.make(slots[1], region(step(0), 0, 32), buf2.at[1], dev[1]).wait_recv()
        here = region(step(0), 0, 32)
        return here[...].astype(F32) + buf2[0].astype(F32) + buf2[1].astype(F32)

    a1 = scatter_start(c_plane_a, ys, ydev, ra1.at[0])
    b1 = scatter_start(c_plane_b, xs, xdev, ra1.at[1])
    a2 = scatter_forward(c_plane_a, ys, ydev, ra1.at[0], ra2.at[0], a1)
    b2 = scatter_forward(c_plane_b, xs, xdev, ra1.at[1], ra2.at[1], b1)
    total = scatter_end(c_plane_a, ys, ydev, ra2.at[0], a2)
    c[:, yy, cc, :32, :] = total.astype(BF16)
    a3 = scatter_start(c_lane_a, xs, xdev, rb1.at[0])
    total = scatter_end(c_plane_b, xs, xdev, ra2.at[1], b2)
    c[xx, :, cc, 32:, :] = total.astype(BF16)
    b3 = scatter_start(c_lane_b, ys, ydev, rb1.at[1])
    a4 = scatter_forward(c_lane_a, xs, xdev, rb1.at[0], rb2.at[0], a3)
    b4 = scatter_forward(c_lane_b, ys, ydev, rb1.at[1], rb2.at[1], b3)
    sums = [
        scatter_end(c_lane_a, xs, xdev, rb2.at[0], a4),
        scatter_end(c_lane_b, ys, ydev, rb2.at[1], b4),
    ]

    for i, total in enumerate(sums):
        lo = total[:, :WIDE_LO].reshape(4, 8, WIDE_LO)
        hi = total[:, WIDE_LO:].reshape(4, 8, block - WIDE_LO)
        hi = jnp.concatenate([hi, jnp.zeros((4, 8, 2 * WIDE_LO - block), F32)], axis=2)
        zout[4 * i : 4 * i + 4] = jnp.concatenate([lo, hi], axis=1).astype(BF16)
    zslots = {}
    for k in range(1, NZ):
        zslots[k] = copies.slot()
        copies.go(zslots[k], zout.at[zs(k)], zback.at[z], (wide, zs(k)))
    zback[z] = zout[z]
    for k in range(1, NZ):
        src = zs(NZ - k)
        copies.make(zslots[k], zout.at[src], zback.at[src], (wide, src)).wait_recv()
    pieces = []
    for n in range(NZ):
        got = zback[n].astype(F32)
        pieces += [got[:8, :], got[8:, : block - WIDE_LO]]
    out[...] = jnp.concatenate(pieces, axis=1).astype(BF16)

    for copy in copies.started:
        copy.wait_send()

    def drain(s, carry):
        def body(d, q):
            rs_copy(d, s, q, first.at[d, q]).wait_send()
            ag_copy(d, s, q, ring(s, d)).wait_send()

        each_sub(body)
        return carry

    lax.fori_loop(0, NZ - 1, drain, 0)


def on_device(tokens, routes, gates, fallback, w_gate, w_up, w_down):
    experts = lax.axis_size("wide")
    narrow = lax.axis_size("narrow")
    tok_rows, width = tokens.shape
    block = width // narrow
    ff = w_gate.shape[2]
    capacity = min(tok_rows // 2, tok_rows * routes.shape[1] // experts)
    rows = experts * narrow * 2 * capacity
    half = rows // 2
    sub = half // SUBS
    cols = ff // narrow

    expert_ids = jnp.arange(experts, dtype=jnp.int32)
    matched = routes[:, :, None] == expert_ids[None, None, :]
    hits = jnp.sum(matched.astype(jnp.int32), axis=1)
    weight_of = jnp.sum(jnp.where(matched, gates[:, :, None], 0.0), axis=1)
    ranks = jnp.cumsum(hits, axis=0) - hits
    primary = jnp.where(ranks < capacity, weight_of, 0.0)
    overflow = jnp.where(ranks < capacity, 0.0, weight_of)
    redirect = fallback[:, None] == expert_ids[None, :]
    weights = primary + jnp.sum(jnp.where(redirect[None], overflow[:, :, None], 0.0), axis=1)
    high = lax.reduce_precision(weights, 8, 7)
    middle = lax.reduce_precision(weights - high, 8, 7)
    low = weights - high - middle
    side = jnp.concatenate([high, middle, low, jnp.zeros_like(low)], axis=1).astype(BF16)
    pieces = tokens.reshape(tok_rows, narrow, block).transpose(1, 0, 2)
    side = jnp.broadcast_to(side[None], (narrow, tok_rows, SIDE))
    tok = jnp.concatenate(
        [pieces[:, :, :WIDE_LO], jnp.concatenate([pieces[:, :, WIDE_LO:], side], axis=2)], axis=1
    )

    vmem = pl.BlockSpec(memory_space=pltpu.VMEM)
    hbm = pl.BlockSpec(memory_space=pl.ANY)
    line = block + SIDE
    copies = 7 + 24 + 4 + 16 + 7
    return pl.pallas_call(
        kernel,
        out_shape=jax.ShapeDtypeStruct((tok_rows, width), BF16),
        in_specs=[vmem, hbm, hbm, hbm],
        out_specs=vmem,
        scratch_shapes=[
            pltpu.VMEM((NZ, 16, WIDE_LO), BF16),
            pltpu.VMEM((NX, NY, NC, 64, line), BF16),
            pltpu.VMEM((rows, block), BF16),
            pltpu.VMEM((8, 256, SIDE), BF16),
            pltpu.VMEM((8, 256, SIDE), F32),
            pltpu.VMEM((block, ff), BF16),
            pltpu.VMEM((block, ff), BF16),
            pltpu.VMEM((ff, block), BF16),
            pltpu.VMEM((2, SUBS, sub, 2 * cols), BF16),
            pltpu.VMEM((2, NZ - 1, SUBS, sub, 2 * cols), BF16),
            pltpu.VMEM((NZ, rows, cols), BF16),
            pltpu.VMEM((rows, block), F32),
            pltpu.VMEM((NX, NY, NC, 64, block), BF16),
            pltpu.VMEM((NX, NY, 64, block), BF16),
            pltpu.VMEM((2, 2, 4, 16, block), BF16),
            pltpu.VMEM((2, 2, 4, 32, block), BF16),
            pltpu.VMEM((2, 2, 16, block), BF16),
            pltpu.VMEM((2, 2, 32, block), BF16),
            pltpu.VMEM((NZ, 16, WIDE_LO), BF16),
            pltpu.VMEM((NZ, 16, WIDE_LO), BF16),
            pltpu.SemaphoreType.DMA((3,)),
            pltpu.SemaphoreType.DMA((copies,)),
            pltpu.SemaphoreType.DMA((copies,)),
            pltpu.SemaphoreType.DMA((2, NZ - 1, SUBS)),
            pltpu.SemaphoreType.DMA((2, NZ - 1, SUBS)),
            pltpu.SemaphoreType.DMA((2, NZ - 1, SUBS)),
            pltpu.SemaphoreType.DMA((2, NZ - 1, SUBS)),
        ],
        compiler_params=pltpu.CompilerParams(
            collective_id=0, has_side_effects=True, vmem_limit_bytes=58 * 1024 * 1024
        ),
        cost_estimate=pl.CostEstimate(
            flops=6 * rows * block * ff, bytes_accessed=6 * block * ff, transcendentals=rows * cols
        ),
        name="experts",
    )(tok, w_gate[0], w_up[0], w_down[0])


def solution(mesh):
    placed = (
        P(("wide", "narrow"), None),
        P(("wide", "narrow"), None),
        P(("wide", "narrow"), None),
        P(),
        P("wide", "narrow", None),
        P("wide", "narrow", None),
        P("wide", None, "narrow"),
    )
    return jax.shard_map(
        on_device,
        mesh=mesh,
        in_specs=placed,
        out_specs=P(("wide", "narrow"), None),
        check_vma=False,
    )
```

time: 391 us -> 197 us (0.50)
  waiting for transfers between devices: 201 us -> 0 us
  Pallas kernels: 0 us -> 188 us
  blocking collectives: 124 us -> 0 us
  matrix products: 28.3 us -> 0 us
  between operations: 13.2 us -> 0.04 us
  local copies, waits for them, and re-layouts: 16.2 us -> 3.29 us
  starting transfers between devices: 4.39 us -> 0 us
    pallas_call x0 -> x1, Pallas kernels: none -> 188 us  [on_device(): pl.pallas_call(kernel, out_shape=jax.ShapeDtypeStruct((tok_rows, width),...]
    all_to_all x3 -> x0, blocking collectives: 124 us -> none  [the longest x1 54.3 us: on_device(): lax.all_to_all(lax.all_to_all(outgoing, 'wide', split_axis=1, concat_axis...]
    reduce_scatter x2 -> x0, waiting for transfers between devices: 96.3 us -> none  [the longest x1 56.5 us: on_device(): lax.psum_scatter(up_part.astype(jnp.bfloat16), 'narrow', scatter_dimensio...]
    all_gather x1 -> x0, waiting for transfers between devices: 58.4 us -> none  [on_device(): lax.all_gather(hidden, 'narrow', axis=1, tiled=True)]
    all_to_all x1 -> x0, waiting for transfers between devices: 45.8 us -> none  [on_device(): lax.all_to_all(lax.all_to_all(going_back, 'wide', split_axis=1, concat_ax...]
    dot_general x7 -> x0, matrix products: 28.3 us -> none  [the longest x1 9.06 us: on_device(): jnp.dot(lax.all_gather(hidden, 'narrow', axis=1, tiled=True), down_w, pre...]
    reshape x4 -> x0, local copies, waits for them, and re-layouts: 7.51 us -> none  [the longest x2 3.76 us: on_device(): going_back = output.reshape(narrow, experts, slots, block)]
    all_to_all x4 -> x0, local copies, waits for them, and re-layouts: 5.37 us -> none  [the longest x1 2.86 us: on_device(): lax.all_to_all(lax.all_to_all(going_back, 'wide', split_axis=1, concat_ax...]
  transfers between devices with their start and end apart: 4 -> 0, of which waited for: 4 -> 0; matrix products, arithmetic and copies ran while one was open for 2% -> 0% of each run, Pallas kernels for 0% -> 0%
where the time goes in v1:
time: 197 us; the launch traced here: 195 us
  Pallas kernels  188 us (95%)
  local copies, waits for them, and re-layouts  3.29 us (2%)
  other arithmetic  3.19 us (2%)
    pallas_call x1, Pallas kernels, on_device(): pl.pallas_call(kernel, out_shape=jax.ShapeDtypeStruct((tok_rows, width),...  188 us

profile of v1, /device:TPU:1, one launch (start us, length us, event | category | flops | bytes accessed | tf_op | source)
XLA Modules:
  0.0 194.7 jit_solution(6710938954690235944)
XLA Ops:
  0.0 0.1 pad.6.clone
  0.1 0.8 select_reduce_fusion.1
  0.9 0.8 convert_reduce_fusion
  1.7 0.7 iota_compare_fusion.1
  2.4 0.1 select_reduce_fusion
  2.6 0.1 maximum_maximum_fusion.1
  2.7 0.8 slice.9
  3.5 0.8 slice.8
  4.3 0.7 maximum_maximum_fusion.tok
  5.0 188.2 %experts.1 = bf16[8,7168]{1,0:T(8,128)(2,1)} custom-call(bf16[8,16,512]{2,1,0:T(8,128)(2,1)} %maximum_maximum_fusion.tok, bf16[896,2048]{1,0:T(8,128)(2,1)} %bitcast.8, bf16[896,2048]{1,0:T(8,128)(2,1)} %bitcast.9, bf16[2048,896]{1,0:T(8,128)(2,1)} %bitcast.10), custom_call_target="tpu_custom_call" | custom-call | flops 11274289152 | bytes 11010048 | tf_op jit(solution)/shard_map/experts/pallas_call | solution.py:464
  193.1 1.6 copy.9
  (6 shorter events, 0.1 us)

commit v2 on v0

v2 whole, which is shorter than its diff:
```python
import functools

import jax
import jax.numpy as jnp
from jax import lax
from jax.experimental import pallas as pl
from jax.experimental.pallas import tpu as pltpu
from jax.sharding import PartitionSpec as P

F32 = jnp.float32
BF16 = jnp.bfloat16
NX, NY, NC, NZ = 4, 4, 2, 8
SIDE = 128
WIDE_LO = 512
GROUPS = 4


def dot(a, b):
    return jnp.dot(a, b, preferred_element_type=F32)


def kernel(
    tok,
    wg_hbm,
    wu_hbm,
    wd_hbm,
    out,
    zin,
    g,
    x,
    sel,
    wcol,
    wg,
    wu,
    wd,
    first,
    part,
    hid,
    acc,
    c,
    core_in,
    land,
    zout,
    zback,
    load_sem,
    z_send,
    z_recv,
    g_send,
    g_recv,
    m_send,
    m_recv,
    rs_send,
    rs_recv,
    ag_send,
    ag_recv,
    cm_send,
    cm_recv,
    r_send,
    r_recv,
    b_send,
    b_recv,
):
    wide, z = lax.axis_index("wide"), lax.axis_index("narrow")
    cc = lax.rem(wide, NC)
    yy = lax.rem(wide // NC, NY)
    xx = wide // (NC * NY)
    block = x.shape[3]
    cols = wg.shape[1] // NZ
    side = g.shape[4] - block

    def at(px, py, pc):
        return (px * NY + py) * NC + pc

    def zs(k):
        return lax.rem(z + k, NZ)

    def chip(k):
        return lax.rem(xx + k // NY, NX), lax.rem(yy + lax.rem(k, NY), NY)

    def chip_back(k):
        return lax.rem(xx + NX - k // NY, NX), lax.rem(yy + NY - lax.rem(k, NY), NY)

    mate = (at(xx, yy, 1 - cc), z)

    def remote(src, dst, send, recv, device):
        return pltpu.make_async_remote_copy(
            src_ref=src,
            dst_ref=dst,
            send_sem=send,
            recv_sem=recv,
            device_id=device,
            device_id_type=pl.DeviceIdType.MESH,
        )

    def loop(lo, hi, body):
        def step(i, carry):
            body(i)
            return carry

        lax.fori_loop(lo, hi, step, 0)

    loads = [
        pltpu.make_async_copy(a, b, load_sem.at[i])
        for i, (a, b) in enumerate(((wg_hbm, wg), (wu_hbm, wu), (wd_hbm, wd)))
    ]
    for load in loads:
        load.start()

    barrier = pltpu.get_barrier_semaphore()

    def greet(device):
        pl.semaphore_signal(barrier, inc=1, device_id=device, device_id_type=pl.DeviceIdType.MESH)

    for k in range(1, NZ):
        greet((wide, zs(k)))
    greet(mate)
    loop(1, NX * NY, lambda k: greet((at(*chip(k), cc), z)))
    pl.semaphore_wait(barrier, NZ - 1 + 1 + NX * NY - 1)

    def z_copy(to):
        return remote(tok.at[to], zin.at[z], z_send.at[to], z_recv.at[z], (wide, to))

    def z_from(src):
        return remote(tok.at[src], zin.at[src], z_send.at[src], z_recv.at[src], (wide, src))

    loop(1, NZ, lambda k: z_copy(zs(k)).start())
    zin[z] = tok[z]

    def group_rows(h):
        return pl.ds(16 * h, 16)

    def g_copy(h, k):
        px, py = chip(k)
        here = g.at[xx, yy, cc, group_rows(h)]
        return remote(here, here, g_send.at[h, k], g_recv.at[h, k], (at(px, py, cc), z))

    def g_from(h, k):
        px, py = chip_back(k)
        there = g.at[px, py, cc, group_rows(h)]
        return remote(there, there, g_send.at[h, k], g_recv.at[h, k], (at(px, py, cc), z))

    def prepare(h):
        for src in (2 * h, 2 * h + 1):
            pl.when(z != src)(lambda src=src: z_from(src).wait_recv())
        arrived = zin[2 * h : 2 * h + 2].astype(F32)
        for half in range(2):
            lanes = slice(half * WIDE_LO, (half + 1) * WIDE_LO)
            value = arrived[:, 8 * half : 8 * half + 8, :].reshape(16, WIDE_LO)
            g[xx, yy, cc, 16 * h : 16 * h + 16, lanes] = value.astype(BF16)
        loop(1, NX * NY, lambda k: g_copy(h, k).start())

    def m_copy(h, core):
        here = g.at[:, :, core, group_rows(h)]
        return remote(here, here, m_send.at[h], m_recv.at[h], mate)

    def share(h):
        loop(1, NX * NY, lambda k: g_from(h, k).wait_recv())
        m_copy(h, cc).start()

    toks, slots = 256, 128

    def select(h):
        lane = lax.broadcasted_iota(jnp.int32, (toks, side), 1)
        row = lax.broadcasted_iota(jnp.int32, (toks, side), 0)
        mine = (lax.rem(lane, 32) == wide) & (lane < 96)
        square_r = lax.broadcasted_iota(jnp.int32, (toks, toks), 0)
        square_c = lax.broadcasted_iota(jnp.int32, (toks, toks), 1)
        lower = ((square_r // 8 == square_c // 8) & (square_c < square_r)).astype(F32).astype(BF16)
        m_copy(h, 1 - cc).wait_recv()
        for d in range(2):
            here = g[2 * d : 2 * d + 2, :, :, 16 * h : 16 * h + 16].reshape(toks, block + side)
            weight = jnp.sum(
                jnp.where(mine, here[:, block:].astype(F32), 0.0), axis=1, keepdims=True
            )
            weight = jnp.broadcast_to(weight, (toks, side))
            chosen = jnp.where(weight > 0.0, 1.0, 0.0)
            rank = dot(lower, chosen.astype(BF16)).astype(jnp.int32)
            place = rank * (toks // 8) + row // 8
            pick = jnp.where((lane == place) & (weight > 0.0), 1.0, 0.0).astype(BF16)
            sel[h, d] = pick
            wcol[h, d] = weight
            taken = lax.dot_general(
                pick, here[:, :block], (((0,), (0,)), ((), ())), preferred_element_type=F32
            )
            x[h, d] = taken.astype(BF16)

    zdev = ((wide, zs(1)), (wide, zs(NZ - 1)))
    pieces = [pl.ds(p * slots // 2, slots // 2) for p in range(2)]

    def ring(s, d):
        return lax.rem(z + NZ - s, NZ) if d == 0 else lax.rem(z + s, NZ)

    def product(h, d, chunk):
        at_cols = pl.ds(pl.multiple_of(chunk * cols, cols), cols)
        return dot(x[h, d], wg[:, at_cols]), dot(x[h, d], wu[:, at_cols])

    def rs_copy(h, d, s, p, src):
        return remote(
            src.at[pieces[p]],
            part.at[h, d, s, pieces[p]],
            rs_send.at[h, d, s, p],
            rs_recv.at[h, d, s, p],
            zdev[d],
        )

    def ag_copy(h, d, s, p, chunk):
        here = hid.at[chunk, h, d, pieces[p]]
        return remote(here, here, ag_send.at[h, d, s, p], ag_recv.at[h, d, s, p], zdev[d])

    def rs_first(h):
        for d in range(2):
            gate, up = product(h, d, ring(1, d))
            first[h, d, :, :cols] = gate.astype(BF16)
            first[h, d, :, cols:] = up.astype(BF16)
            for p in range(2):
                rs_copy(h, d, 0, p, first.at[h, d]).start()

    def rs_step(h, s):
        for d in range(2):
            gate, up = product(h, d, ring(s + 1, d))
            for p in range(2):
                rows = slice(p * slots // 2, (p + 1) * slots // 2)
                rs_copy(h, d, s - 1, p, first.at[h, d]).wait_recv()
                here = part.at[h, d, s - 1, pieces[p]]
                here[:, :cols] = (here[:, :cols].astype(F32) + gate[rows]).astype(BF16)
                here[:, cols:] = (here[:, cols:].astype(F32) + up[rows]).astype(BF16)
                rs_copy(h, d, s, p, part.at[h, d, s - 1]).start()

    def down(h, d, chunk):
        at_cols = pl.ds(pl.multiple_of(chunk * cols, cols), cols)
        return dot(hid[chunk, h, d], wd[at_cols, :])

    def rs_last(h):
        for d in range(2):
            gate, up = product(h, d, z)
            for p in range(2):
                rows = slice(p * slots // 2, (p + 1) * slots // 2)
                rs_copy(h, d, NZ - 2, p, first.at[h, d]).wait_recv()
                here = part.at[h, d, NZ - 2, pieces[p]]
                gates = gate[rows] + here[:, :cols].astype(F32)
                ups = up[rows] + here[:, cols:].astype(F32)
                hid[z, h, d, pieces[p], :] = (gates / (1.0 + jnp.exp(-gates)) * ups).astype(BF16)
                ag_copy(h, d, 0, p, z).start()
        for d in range(2):
            acc[h, d] = down(h, d, z)

    def ag_step(h, s):
        for d in range(2):
            for p in range(2):
                ag_copy(h, d, s - 1, p, ring(s, d)).wait_recv()
                ag_copy(h, d, s, p, ring(s, d)).start()
        for d in range(2):
            acc[h, d] = acc[h, d] + down(h, d, ring(s, d))

    def cm_copy(h, core):
        return remote(c.at[h, :, :, core], core_in.at[h], cm_send.at[h], cm_recv.at[h], mate)

    def ag_last(h):
        for d in range(2):
            chunk = ring(NZ - 1, d)
            for p in range(2):
                ag_copy(h, d, NZ - 2, p, chunk).wait_recv()
            expert_out = (acc[h, d] + down(h, d, chunk)).astype(BF16)
            mixed = dot(sel[h, d], expert_out) * wcol[h, d][:, :1]
            c[h, 2 * d : 2 * d + 2] = mixed.astype(BF16).reshape(2, NY, NC, 16, block)
        cm_copy(h, 1 - cc).start()

    def r_copy(h, k):
        px, py = chip(k)
        return remote(
            c.at[h, px, py, cc],
            land.at[h, xx, yy],
            r_send.at[h, k],
            r_recv.at[h, k],
            (at(px, py, cc), z),
        )

    def r_from(h, k):
        px, py = chip_back(k)
        return remote(
            c.at[h, px, py, cc],
            land.at[h, px, py],
            r_send.at[h, k],
            r_recv.at[h, k],
            (at(px, py, cc), z),
        )

    def spread(h):
        cm_copy(h, cc).wait_recv()
        for px in range(NX):
            both = c[h, px, :, cc].astype(F32) + core_in[h, px].astype(F32)
            c[h, px, :, cc] = both.astype(BF16)
        land[h, xx, yy] = c[h, xx, yy, cc]
        loop(1, NX * NY, lambda k: r_copy(h, k).start())

    def b_copy(h, j):
        to = 2 * h + j
        return remote(zout.at[h, j], zback.at[z], b_send.at[h, j], b_recv.at[z], (wide, to))

    def collect(h):
        loop(1, NX * NY, lambda k: r_from(h, k).wait_recv())
        total = jnp.sum(land[h].reshape(NX * NY, 16, block).astype(F32), axis=0)
        lo = total[:, :WIDE_LO].reshape(2, 8, WIDE_LO)
        hi = total[:, WIDE_LO:].reshape(2, 8, block - WIDE_LO)
        hi = jnp.concatenate([hi, jnp.zeros((2, 8, 2 * WIDE_LO - block), F32)], axis=2)
        zout[h] = jnp.concatenate([lo, hi], axis=1).astype(BF16)
        for j in range(2):
            pl.when(z != 2 * h + j)(lambda j=j: b_copy(h, j).start())

            @pl.when(z == 2 * h + j)
            def _(j=j):
                zback[z] = zout[h, j]

    for h in range(GROUPS):
        prepare(h)
    loads[0].wait()
    loads[1].wait()
    for h in range(2):
        share(h)
        select(h)
        rs_first(h)

    def rs_pair(s):
        rs_step(0, s)
        rs_step(1, s)

    loop(1, 3, rs_pair)
    share(2)
    loop(3, 4, rs_pair)
    select(2)
    loop(4, 5, rs_pair)
    share(3)
    loop(5, 6, rs_pair)
    select(3)
    loop(6, NZ - 1, rs_pair)
    loads[2].wait()
    for h in range(2):
        rs_last(h)
        rs_first(h + 2)

    def both_pairs(s):
        for h in range(2):
            ag_step(h, s)
            rs_step(h + 2, s)

    loop(1, NZ - 1, both_pairs)
    for h in range(2):
        ag_last(h)
        rs_last(h + 2)

    def ag_pair(s):
        ag_step(2, s)
        ag_step(3, s)

    loop(1, 3, ag_pair)
    spread(0)
    loop(3, 4, ag_pair)
    spread(1)
    loop(4, 5, ag_pair)
    collect(0)
    loop(5, 6, ag_pair)
    collect(1)
    loop(6, NZ - 1, ag_pair)
    ag_last(2)
    ag_last(3)
    spread(2)
    spread(3)
    collect(2)
    collect(3)

    def b_from(src):
        return remote(
            zout.at[0, 0], zback.at[src], b_send.at[0, 0], b_recv.at[src], (wide, src)
        )

    loop(1, NZ, lambda k: b_from(zs(k)).wait_recv())
    line = []
    for n in range(NZ):
        got = zback[n].astype(F32)
        line += [got[:8, :], got[8:, : block - WIDE_LO]]
    out[...] = jnp.concatenate(line, axis=1).astype(BF16)

    loop(1, NZ, lambda k: z_copy(zs(k)).wait_send())
    for h in range(GROUPS):
        loop(1, NX * NY, lambda k: g_copy(h, k).wait_send())
        m_copy(h, cc).wait_send()
        cm_copy(h, 1 - cc).wait_send()
        loop(1, NX * NY, lambda k: r_copy(h, k).wait_send())
        for j in range(2):
            pl.when(z != 2 * h + j)(lambda j=j: b_copy(h, j).wait_send())

    def drain(s):
        for h in range(GROUPS):
            for d in range(2):
                for p in range(2):
                    rs_copy(h, d, s, p, first.at[h, d]).wait_send()
                    ag_copy(h, d, s, p, ring(s, d)).wait_send()

    loop(0, NZ - 1, drain)


def on_device(tokens, routes, gates, fallback, w_gate, w_up, w_down):
    experts = lax.axis_size("wide")
    narrow = lax.axis_size("narrow")
    tok_rows, width = tokens.shape
    block = width // narrow
    ff = w_gate.shape[2]
    capacity = min(tok_rows // 2, tok_rows * routes.shape[1] // experts)
    rows = experts * narrow * 2 * capacity
    cols = ff // narrow
    slots = rows // (2 * GROUPS)

    expert_ids = jnp.arange(experts, dtype=jnp.int32)
    matched = routes[:, :, None] == expert_ids[None, None, :]
    hits = jnp.sum(matched.astype(jnp.int32), axis=1)
    weight_of = jnp.sum(jnp.where(matched, gates[:, :, None], 0.0), axis=1)
    ranks = jnp.cumsum(hits, axis=0) - hits
    primary = jnp.where(ranks < capacity, weight_of, 0.0)
    overflow = jnp.where(ranks < capacity, 0.0, weight_of)
    redirect = fallback[:, None] == expert_ids[None, :]
    weights = primary + jnp.sum(jnp.where(redirect[None], overflow[:, :, None], 0.0), axis=1)
    high = lax.reduce_precision(weights, 8, 7)
    middle = lax.reduce_precision(weights - high, 8, 7)
    low = weights - high - middle
    side = jnp.concatenate([high, middle, low, jnp.zeros_like(low)], axis=1).astype(BF16)
    pieces = tokens.reshape(tok_rows, narrow, block).transpose(1, 0, 2)
    side = jnp.broadcast_to(side[None], (narrow, tok_rows, SIDE))
    tok = jnp.concatenate(
        [pieces[:, :, :WIDE_LO], jnp.concatenate([pieces[:, :, WIDE_LO:], side], axis=2)], axis=1
    )

    vmem = pl.BlockSpec(memory_space=pltpu.VMEM)
    hbm = pl.BlockSpec(memory_space=pl.ANY)
    line = block + SIDE
    dma = pltpu.SemaphoreType.DMA
    return pl.pallas_call(
        kernel,
        out_shape=jax.ShapeDtypeStruct((tok_rows, width), BF16),
        in_specs=[vmem, hbm, hbm, hbm],
        out_specs=vmem,
        scratch_shapes=[
            pltpu.VMEM((NZ, 16, WIDE_LO), BF16),
            pltpu.VMEM((NX, NY, NC, 64, line), BF16),
            pltpu.VMEM((GROUPS, 2, slots, block), BF16),
            pltpu.VMEM((GROUPS, 2, 256, slots), BF16),
            pltpu.VMEM((GROUPS, 2, 256, SIDE), F32),
            pltpu.VMEM((block, ff), BF16),
            pltpu.VMEM((block, ff), BF16),
            pltpu.VMEM((ff, block), BF16),
            pltpu.VMEM((GROUPS, 2, slots, 2 * cols), BF16),
            pltpu.VMEM((GROUPS, 2, NZ - 1, slots, 2 * cols), BF16),
            pltpu.VMEM((NZ, GROUPS, 2, slots, cols), BF16),
            pltpu.VMEM((GROUPS, 2, slots, block), F32),
            pltpu.VMEM((GROUPS, NX, NY, NC, 16, block), BF16),
            pltpu.VMEM((GROUPS, NX, NY, 16, block), BF16),
            pltpu.VMEM((GROUPS, NX, NY, 16, block), BF16),
            pltpu.VMEM((GROUPS, 2, 16, WIDE_LO), BF16),
            pltpu.VMEM((NZ, 16, WIDE_LO), BF16),
            dma((3,)),
            dma((NZ,)),
            dma((NZ,)),
            dma((GROUPS, NX * NY)),
            dma((GROUPS, NX * NY)),
            dma((GROUPS,)),
            dma((GROUPS,)),
            dma((GROUPS, 2, NZ - 1, 2)),
            dma((GROUPS, 2, NZ - 1, 2)),
            dma((GROUPS, 2, NZ - 1, 2)),
            dma((GROUPS, 2, NZ - 1, 2)),
            dma((GROUPS,)),
            dma((GROUPS,)),
            dma((GROUPS, NX * NY)),
            dma((GROUPS, NX * NY)),
            dma((GROUPS, 2)),
            dma((NZ,)),
        ],
        compiler_params=pltpu.CompilerParams(
            collective_id=0, has_side_effects=True, vmem_limit_bytes=58 * 1024 * 1024
        ),
        cost_estimate=pl.CostEstimate(
            flops=6 * rows * block * ff, bytes_accessed=6 * block * ff, transcendentals=rows * cols
        ),
        name="experts",
    )(tok, w_gate[0], w_up[0], w_down[0])


def solution(mesh):
    placed = (
        P(("wide", "narrow"), None),
        P(("wide", "narrow"), None),
        P(("wide", "narrow"), None),
        P(),
        P("wide", "narrow", None),
        P("wide", "narrow", None),
        P("wide", None, "narrow"),
    )
    return jax.shard_map(
        on_device,
        mesh=mesh,
        in_specs=placed,
        out_specs=P(("wide", "narrow"), None),
        check_vma=False,
    )
```

time: 391 us -> 191 us (0.49)
  waiting for transfers between devices: 201 us -> 0 us
  Pallas kernels: 0 us -> 184 us
  blocking collectives: 124 us -> 0 us
  matrix products: 28.3 us -> 0 us
  between operations: 13.2 us -> 0.05 us
  local copies, waits for them, and re-layouts: 16.2 us -> 3.29 us
  starting transfers between devices: 4.39 us -> 0 us
    pallas_call x0 -> x1, Pallas kernels: none -> 184 us  [on_device(): pl.pallas_call(kernel, out_shape=jax.ShapeDtypeStruct((tok_rows, width),...]
    all_to_all x3 -> x0, blocking collectives: 124 us -> none  [the longest x1 54.3 us: on_device(): lax.all_to_all(lax.all_to_all(outgoing, 'wide', split_axis=1, concat_axis...]
    reduce_scatter x2 -> x0, waiting for transfers between devices: 96.3 us -> none  [the longest x1 56.5 us: on_device(): lax.psum_scatter(up_part.astype(jnp.bfloat16), 'narrow', scatter_dimensio...]
    all_gather x1 -> x0, waiting for transfers between devices: 58.4 us -> none  [on_device(): lax.all_gather(hidden, 'narrow', axis=1, tiled=True)]
    all_to_all x1 -> x0, waiting for transfers between devices: 45.8 us -> none  [on_device(): lax.all_to_all(lax.all_to_all(going_back, 'wide', split_axis=1, concat_ax...]
    dot_general x7 -> x0, matrix products: 28.3 us -> none  [the longest x1 9.06 us: on_device(): jnp.dot(lax.all_gather(hidden, 'narrow', axis=1, tiled=True), down_w, pre...]
    reshape x4 -> x0, local copies, waits for them, and re-layouts: 7.51 us -> none  [the longest x2 3.76 us: on_device(): going_back = output.reshape(narrow, experts, slots, block)]
    all_to_all x4 -> x0, local copies, waits for them, and re-layouts: 5.37 us -> none  [the longest x1 2.86 us: on_device(): lax.all_to_all(lax.all_to_all(going_back, 'wide', split_axis=1, concat_ax...]
  transfers between devices with their start and end apart: 4 -> 0, of which waited for: 4 -> 0; matrix products, arithmetic and copies ran while one was open for 2% -> 0% of each run, Pallas kernels for 0% -> 0%
where the time goes in v2:
time: 191 us; the launch traced here: 190 us
  Pallas kernels  184 us (96%)
  local copies, waits for them, and re-layouts  3.29 us (2%)
  other arithmetic  3.19 us (2%)
    pallas_call x1, Pallas kernels, on_device(): pl.pallas_call(kernel, out_shape=jax.ShapeDtypeStruct((tok_rows, width),...  184 us

profile of v2, /device:TPU:1, one launch (start us, length us, event | category | flops | bytes accessed | tf_op | source)
XLA Modules:
  0.0 190.2 jit_solution(10511347893135518677)
XLA Ops:
  0.0 0.1 pad.6.clone
  0.1 0.8 select_reduce_fusion.1
  0.9 0.8 convert_reduce_fusion
  1.7 0.7 iota_compare_fusion.1
  2.4 0.1 select_reduce_fusion
  2.6 0.1 maximum_maximum_fusion.1
  2.7 0.8 slice.9
  3.5 0.8 slice.8
  4.3 0.7 maximum_maximum_fusion.tok
  5.0 183.7 %experts.1 = bf16[8,7168]{1,0:T(8,128)(2,1)} custom-call(bf16[8,16,512]{2,1,0:T(8,128)(2,1)} %maximum_maximum_fusion.tok, bf16[896,2048]{1,0:T(8,128)(2,1)} %bitcast.8, bf16[896,2048]{1,0:T(8,128)(2,1)} %bitcast.9, bf16[2048,896]{1,0:T(8,128)(2,1)} %bitcast.10), custom_call_target="tpu_custom_call" | custom-call | flops 11274289152 | bytes 11010048 | tf_op jit(solution)/shard_map/experts/pallas_call | solution.py:436
  188.7 1.6 copy.9
  (6 shorter events, 0.1 us)
